TPU v7x, 32 devices: a whole 2x2x4 slice. The times are simulated.
32 devices in a mesh: dp: 8 (over z, y), fsdp: 4 (over x, core).
Axes of the slice: x: 2, y: 2, z: 4, core: 2. Of those that a mesh axis runs over, the one named last changes fastest.
Arguments:
- feats: bfloat16 [8, 4, 8, 128, 256], P('dp', 'fsdp'), may hold values from -6 to 6
- grad_out: bfloat16 [8, 4, 8, 128, 256], P('dp', 'fsdp'), may hold values from -6 to 6
- kernel: bfloat16 [27, 256, 256], P(None, 'fsdp'), may hold values from -0.25 to 0.25
- send_bricks: int32 [8, 4, 8, 2], P('dp', 'fsdp'), may hold values from -1 to 7, as said below
- kmap: int32 [8, 4, 27, 2, 3], P('dp', 'fsdp'), may hold values from 0 to 23, as said below
- pair_count: int32 [8, 4, 27], P('dp', 'fsdp'), may hold values from 1 to 3, as said below
Outputs:
- out_feats: bfloat16 [8, 4, 8, 128, 256], P('dp', 'fsdp')
- in_grad: bfloat16 [8, 4, 8, 128, 256], P('dp', 'fsdp')
- kernel_grad: float32 [27, 256, 256], P(None, 'fsdp')
Inputs may be any that keep to these rules, and one draw needn't show every extreme that they name: `send_bricks`: entry (d, f, p, c) names the brick of device (d, f) sent to device (p, f) in slot c, or -1 for an empty slot. A device sends nothing to itself, fills exactly 6 slots, and fills both slots of at least one peer. kmap[d, f, t, 0, s] is an input brick of pool[d, f]: below 8 an own brick, else received slot p * 2 + c after the 8 own ones, and then always a slot that its sender filled. kmap[d, f, t, 1, s] is an output brick, below 8. Slots that are not live hold such ids too. `pair_count`: on some device every offset has 3 live slots.
All inputs are finite; a program needn't handle non-finite values.
Results may differ from a plain program's by a relative error of at most 0.0046.
Values may be sent and summed in bfloat16 or wider, within the bound.
A program may use at most 192 MiB of HBM per device.

v0:
```python
import jax
import jax.numpy as jnp
from jax import lax
from jax.sharding import PartitionSpec as P


def on_device(feats, grad_out, kernel, send_bricks, kmap, pair_count):
    own_rows = feats[0, 0]
    upstream_rows = grad_out[0, 0]
    senders = send_bricks[0, 0]
    peer_total = senders.shape[0]
    slot_cap = senders.shape[1]
    brick_total = own_rows.shape[0]
    brick_rows = own_rows.shape[1]
    channels = own_rows.shape[2]
    filled = senders >= 0
    outgoing = own_rows[jnp.maximum(senders, 0)] * filled[:, :, None, None].astype(jnp.bfloat16)
    incoming = lax.all_to_all(outgoing, "dp", split_axis=0, concat_axis=0, tiled=True)
    weights = lax.all_gather(kernel, "fsdp", axis=1, tiled=True)
    pool = jnp.concatenate(
        [own_rows, incoming.reshape(peer_total * slot_cap, brick_rows, channels)], axis=0
    )
    pool_total = pool.shape[0]
    source_map = kmap[0, 0, :, 0, :]
    target_map = kmap[0, 0, :, 1, :]
    counts = pair_count[0, 0]
    tap_total = source_map.shape[0]
    slot_total = source_map.shape[1]
    active = (jnp.arange(slot_total)[None, :] < counts[:, None]).astype(jnp.bfloat16)
    inputs = pool[source_map] * active[:, :, None, None]
    upstream = upstream_rows[target_map] * active[:, :, None, None]
    contrib = jnp.einsum("tsvc,tcd->tsvd", inputs, weights, preferred_element_type=jnp.float32)
    produced = jax.ops.segment_sum(
        contrib.reshape(tap_total * slot_total, brick_rows, channels),
        target_map.reshape(-1),
        num_segments=brick_total,
    )
    backward = jnp.einsum("tsvd,tcd->tsvc", upstream, weights, preferred_element_type=jnp.float32)
    pool_grad = jax.ops.segment_sum(
        backward.reshape(tap_total * slot_total, brick_rows, channels),
        source_map.reshape(-1),
        num_segments=pool_total,
    )
    partial_value = jnp.einsum(
        "tsvc,tsvd->tcd", inputs, upstream, preferred_element_type=jnp.float32
    )
    ghosts = (
        pool_grad[brick_total:]
        .astype(jnp.bfloat16)
        .reshape(peer_total, slot_cap, brick_rows, channels)
    )
    returned = lax.all_to_all(ghosts, "dp", split_axis=0, concat_axis=0, tiled=True)
    owners = jnp.where(filled, senders, brick_total).reshape(-1)
    gathered_back = jax.ops.segment_sum(
        returned.reshape(peer_total * slot_cap, brick_rows, channels).astype(jnp.float32),
        owners,
        num_segments=brick_total + 1,
    )[:brick_total]
    in_grad = (pool_grad[:brick_total] + gathered_back).astype(jnp.bfloat16)
    divisor = jnp.float32(4 * lax.axis_size("dp") * lax.axis_size("fsdp"))
    portion = lax.psum_scatter(partial_value, "fsdp", scatter_dimension=1, tiled=True)
    portion = lax.psum(portion, "dp")
    kernel_grad = portion / divisor
    return (produced.astype(jnp.bfloat16)[None, None], in_grad[None, None], kernel_grad)


def solution(mesh):
    placed = (
        P("dp", "fsdp", None, None, None),
        P("dp", "fsdp", None, None, None),
        P(None, "fsdp", None),
        P("dp", "fsdp", None, None),
        P("dp", "fsdp", None, None, None),
        P("dp", "fsdp", None),
    )
    return jax.shard_map(
        on_device,
        mesh=mesh,
        in_specs=placed,
        out_specs=(
            P("dp", "fsdp", None, None, None),
            P("dp", "fsdp", None, None, None),
            P(None, "fsdp", None),
        ),
        check_vma=False,
    )
```

profile of v0, /device:TPU:12, one launch (start us, length us, event | category | flops | bytes accessed | tf_op | source)
XLA Modules:
  0.0 236.4 jit_solution(2049440299937820528)
XLA Ops:
  8.8 0.7 fusion.20
  9.6 1.7 gather_fusion
  11.2 1.1 broadcast_multiply_fusion.1
  12.3 6.2 %all-to-all-start = ((bf16[8,2,128,256]{3,2,1,0:T(8,128)(2,1)}), bf16[8,2,128,256]{3,2,1,0:T(8,128)(2,1)S(1)}, u32[]{:S(2)}, u32[]{:S(2)}) async-start(bf16[8,2,128,256]{3,2,1,0:T(8,128)(2,1)} %broadcast_multiply_fusion.1), calls=%async_computation | async-start | bytes 2097152 | tf_op jit(solution)/shard_map/all_to_all | solution.py:18
  18.8 5.7 %gather_fusion.2 = bf16[81,128,256]{2,1,0:T(8,128)(2,1)} fusion(bf16[8,128,256]{2,1,0:T(8,128)(2,1)S(1)} %bitcast.47, s32[1024]{0:T(1024)S(1)} %pad_clamp_fusion), kind=kCustom, calls=%fused_computation.2 | custom fusion | bytes 10617156 | tf_op jit(solution)/shard_map/gather | solution.py:31
  24.5 8.1 %copy.28 = bf16[27,3,128,256]{2,3,1,0:T(8,128)(2,1)} copy(bf16[27,3,128,256]{3,2,1,0:T(8,128)(2,1)} %bitcast.51) | data formatting | bytes 10616832 | tf_op jit(solution)/shard_map/gather | solution.py:31
  32.8 8.2 %all-to-all-done = bf16[8,2,128,256]{3,2,1,0:T(8,128)(2,1)S(1)} async-done(((bf16[8,2,128,256]{3,2,1,0:T(8,128)(2,1)}), bf16[8,2,128,256]{3,2,1,0:T(8,128)(2,1)S(1)}, u32[]{:S(2)}, u32[]{:S(2)}) %all-to-all-start) | async-done | bytes 1048608 | tf_op jit(solution)/shard_map/all_to_all | solution.py:18
  41.2 5.7 %gather_fusion.1 = bf16[81,128,256]{2,1,0:T(8,128)(2,1)} fusion(bf16[24,128,256]{2,1,0:T(8,128)(2,1)S(1)} %pad_maximum_fusion, s32[1024]{0:T(1024)S(1)} %pad_clamp_fusion.1), kind=kCustom, calls=%fused_computation.1 | custom fusion | bytes 10617156 | tf_op jit(solution)/shard_map/gather | solution.py:30
  46.8 8.0 %copy.24 = bf16[27,3,128,256]{2,3,1,0:T(8,128)(2,1)} copy(bf16[27,3,128,256]{3,2,1,0:T(8,128)(2,1)} %bitcast.50) | data formatting | bytes 10616832 | tf_op jit(solution)/shard_map/gather | solution.py:30
  54.8 9.1 %fusion.9 = f32[27,256,256]{2,1,0:T(8,128)} fusion(bf16[27,3,128,256]{2,3,1,0:T(8,128)(2,1)} %copy.28, bf16[27,3,128,256]{2,3,1,0:T(8,128)(2,1)} %copy.24, bf16[27,3]{1,0:T(8,128)(2,1)S(1)} %fusion.19), kind=kOutput, calls=%fused_computation.15 | convolution fusion | flops 1364262912 | bytes 17694882 | tf_op jit(solution)/shard_map/tsvc,tsvd->tcd/dot_general | solution.py:44
  64.2 10.6 %fusion.2 = f32[27,3,128,256]{3,2,1,0:T(8,128)} fusion(bf16[27,3,128,256]{2,3,1,0:T(8,128)(2,1)} %copy.28, bf16[27,256,256]{2,1,0:T(8,128)(2,1)} %all-gather.2.cloned.1.call-done, bf16[27,3]{1,0:T(8,128)(2,1)S(1)} %fusion.19), kind=kOutput, calls=%fused_computation.8 | convolution fusion | flops 1361608704 | bytes 19464354 | tf_op jit(solution)/shard_map/tsvd,tcd->tsvc/dot_general | solution.py:38
  74.8 2.3 broadcast_in_dim.26
  77.1 29.1 %scatter_fusion.1 = f32[24,128,256]{2,1,0:T(8,128)} fusion(f32[24,128,256]{2,1,0:T(8,128)} %broadcast_in_dim.26, s32[81]{0:T(128)S(1)} %reshape.184, f32[81,128,256]{2,1,0:T(8,128)} %bitcast.49), kind=kCustom, calls=%fused_computation.4 | custom fusion | flops 2654208 | bytes 31850820 | tf_op jit(solution)/shard_map/scatter-add | solution.py:39
  106.1 2.7 %slice.41 = bf16[16,128,256]{2,1,0:T(8,128)(2,1)} slice(f32[24,128,256]{2,1,0:T(8,128)} %scatter_fusion.1), slice={[8:24], [0:128], [0:256]} | slice | bytes 2097152 | tf_op jit(solution)/shard_map/slice | solution.py:48
  108.8 7.3 %all-to-all-start.1 = ((bf16[8,2,128,256]{3,2,1,0:T(8,128)(2,1)}), bf16[8,2,128,256]{3,2,1,0:T(8,128)(2,1)S(1)}, u32[]{:S(2)}, u32[]{:S(2)}) async-start(bf16[8,2,128,256]{3,2,1,0:T(8,128)(2,1)} %bitcast.17), calls=%async_computation.1 | async-start | bytes 2097152 | tf_op jit(solution)/shard_map/all_to_all | solution.py:52
  116.5 13.0 %reduce-scatter.2.cloned.1.call-done = f32[27,64,256]{2,1,0:T(8,128)} async-done(((f32[27,256,256]{2,1,0:T(8,128)}), f32[27,64,256]{2,1,0:T(8,128)}) %reduce-scatter.2.cloned.1.call-update) | async-done | bytes 1769488 | tf_op jit(solution)/shard_map/reduce_scatter | solution.py:61
  129.6 9.3 %fusion.5 = f32[27,3,128,256]{3,2,1,0:T(8,128)} fusion(bf16[27,3,128,256]{2,3,1,0:T(8,128)(2,1)} %copy.24, bf16[27,256,256]{2,1,0:T(8,128)(2,1)} %all-gather.2.cloned.1.call-done, bf16[27,3]{1,0:T(8,128)(2,1)S(1)} %fusion.19), kind=kOutput, calls=%fused_computation.11 | convolution fusion | flops 1361608704 | bytes 19464354 | tf_op jit(solution)/shard_map/tsvc,tcd->tsvd/dot_general | solution.py:32
  139.0 17.7 %scatter_fusion = f32[8,128,256]{2,1,0:T(8,128)S(1)} fusion(f32[8,128,256]{2,1,0:T(8,128)S(1)} %broadcast_in_dim.12, s32[81]{0:T(128)S(1)} %reshape.176, f32[81,128,256]{2,1,0:T(8,128)} %bitcast.48), kind=kCustom, calls=%fused_computation.3 | custom fusion | flops 2654208 | bytes 31850820 | tf_op jit(solution)/shard_map/scatter-add | solution.py:33
  156.6 0.8 convert_bitcast_fusion
  157.5 1.7 bitcast_convert_fusion
  159.2 3.5 %scatter_fusion.2 = f32[9,128,256]{2,1,0:T(8,128)S(1)} fusion(f32[9,128,256]{2,1,0:T(8,128)S(1)} %broadcast_in_dim.27, s32[16]{0:T(128)S(1)} %fusion.21, f32[16,128,256]{2,1,0:T(8,128)} %bitcast_convert_fusion), kind=kCustom, calls=%fused_computation.5 | custom fusion | flops 524288 | bytes 6291520 | tf_op jit(solution)/shard_map/scatter-add | solution.py:54
  162.8 2.1 fusion.18
  164.9 62.1 %all-reduce.2.cloned.1.call-done = f32[27,64,256]{2,1,0:T(8,128)} async-done(((f32[27,64,256]{2,1,0:T(8,128)}), f32[27,64,256]{2,1,0:T(8,128)}) %all-reduce.2.cloned.1.call-update) | async-done | bytes 1769488 | tf_op jit(solution)/shard_map/psum | solution.py:62
  227.0 2.9 %broadcast_multiply_fusion = f32[27,64,256]{2,1,0:T(8,128)} fusion(f32[27,64,256]{2,1,0:T(8,128)} %all-reduce.2.cloned.1.call-done), kind=kLoop, calls=%fused_computation.24 | loop fusion | flops 442368 | bytes 3538944 | tf_op jit(solution)/shard_map/div | solution.py:63
  (44 shorter events, 3.1 us)
Async XLA Ops:
  7.2 11.6 %copy-start = (bf16[1,1,8,128,256]{4,3,2,1,0:T(8,128)(2,1)S(1)}, bf16[1,1,8,128,256]{4,3,2,1,0:T(8,128)(2,1)}, u32[]{:S(2)}) copy-start(bf16[1,1,8,128,256]{4,3,2,1,0:T(8,128)(2,1)} %param.7) | copy-start | bytes 1572868
  7.2 11.4 %copy-start.3 = (s32[1,1,27,2,3]{2,3,4,1,0:T(2,128)S(1)}, s32[1,1,27,2,3]{2,3,4,1,0:T(2,128)}, u32[]{:S(2)}) copy-start(s32[1,1,27,2,3]{2,3,4,1,0:T(2,128)} %param.10) | copy-start | bytes 1948
  7.2 57.0 %all-gather.2.cloned.1.call-start = ((), (), s32[]{:S(2)}) async-start(), calls=%async_computation.3 | async-start | bytes 4423680 | tf_op jit(solution)/shard_map/all_gather | solution.py:19
  12.3 28.7 %all-to-all-start = ((bf16[8,2,128,256]{3,2,1,0:T(8,128)(2,1)}), bf16[8,2,128,256]{3,2,1,0:T(8,128)(2,1)S(1)}, u32[]{:S(2)}, u32[]{:S(2)}) async-start(bf16[8,2,128,256]{3,2,1,0:T(8,128)(2,1)} %broadcast_multiply_fusion.1), calls=%async_computation | async-start | bytes 2097152 | tf_op jit(solution)/shard_map/all_to_all | solution.py:18
  18.6 111.0 %reduce-scatter.2.cloned.1.call-start = ((), (), s32[]{:S(2)}) async-start(), calls=%async_computation.4 | async-start | bytes 8847360 | tf_op jit(solution)/shard_map/reduce_scatter | solution.py:61
  24.5 8.3 %copy-start.5 = (s32[1,1,27]{2,1,0:T(1,128)S(1)}, s32[1,1,27]{2,1,0:T(1,128)}, u32[]{:S(2)}) copy-start(s32[1,1,27]{2,1,0:T(1,128)} %param.11) | copy-start | bytes 328
  24.5 16.5 %copy-start.2 = (bf16[1,1,8,128,256]{4,3,2,1,0:T(8,128)(2,1)S(1)}, bf16[1,1,8,128,256]{4,3,2,1,0:T(8,128)(2,1)}, u32[]{:S(2)}) copy-start(bf16[1,1,8,128,256]{4,3,2,1,0:T(8,128)(2,1)} %param.6) | copy-start | bytes 1572868
  77.1 39.1 %copy-start.4 = (s32[1,1,8,2]{2,3,1,0:T(2,128)S(1)}, s32[1,1,8,2]{2,3,1,0:T(2,128)}, u32[]{:S(2)}) copy-start(s32[1,1,8,2]{2,3,1,0:T(2,128)} %param.9) | copy-start | bytes 196
  108.8 48.7 %all-to-all-start.1 = ((bf16[8,2,128,256]{3,2,1,0:T(8,128)(2,1)}), bf16[8,2,128,256]{3,2,1,0:T(8,128)(2,1)S(1)}, u32[]{:S(2)}, u32[]{:S(2)}) async-start(bf16[8,2,128,256]{3,2,1,0:T(8,128)(2,1)} %bitcast.17), calls=%async_computation.1 | async-start | bytes 2097152 | tf_op jit(solution)/shard_map/all_to_all | solution.py:52
  116.1 110.9 %all-reduce.2.cloned.1.call-start = ((), (), s32[]{:S(2)}) async-start(), calls=%async_computation.5 | async-start | bytes 3538944 | tf_op jit(solution)/shard_map/psum | solution.py:62
  159.1 70.7 %copy-start.1 = (bf16[1,1,8,128,256]{4,3,2,1,0:T(8,128)(2,1)S(1)}, bf16[1,1,8,128,256]{4,3,2,1,0:T(8,128)(2,1)}, u32[]{:S(2)}) copy-start(bf16[1,1,8,128,256]{4,3,2,1,0:T(8,128)(2,1)} %param.7) | copy-start | bytes 1572868
Sparse Core Ops, SparseCore 0:
  9.6 31.8 all-gather.1
  64.1 65.4 reduce-scatter.1
  133.5 93.4 all-reduce.1
where the time goes:
time: 239 us; the launch traced here: 236 us
  waiting for transfers between devices  84.1 us (35%)
  other arithmetic  60.4 us (25%)
  local copies, waits for them, and re-layouts  35.5 us (15%)
  matrix products  29 us (12%)
  between operations  13.9 us (6%)
  starting transfers between devices  13.5 us (6%)
    psum x1, waiting for transfers between devices, on_device(): portion = lax.psum(portion, 'dp')  62.1 us
    scatter-add x1, other arithmetic, on_device(): jax.ops.segment_sum(backward.reshape(tap_total * slot_total, brick_rows,...  29.1 us
    scatter-add x1, other arithmetic, on_device(): jax.ops.segment_sum(contrib.reshape(tap_total * slot_total, brick_rows, c...  17.7 us
    gather x2, local copies, waits for them, and re-layouts, on_device(): upstream = upstream_rows[target_map] * active[:, :, None, None]  13.7 us
    gather x2, local copies, waits for them, and re-layouts, on_device(): inputs = pool[source_map] * active[:, :, None, None]  13.7 us
    reduce_scatter x1, waiting for transfers between devices, on_device(): lax.psum_scatter(partial_value, 'fsdp', scatter_dimension=1, tiled=True)  13 us
    dot_general x1, matrix products, on_device(): jnp.einsum('tsvd,tcd->tsvc', upstream, weights, preferred_element_type=jn...  10.6 us
    dot_general x1, matrix products, on_device(): jnp.einsum('tsvc,tcd->tsvd', inputs, weights, preferred_element_type=jnp....  9.33 us
  transfers between devices with their start and end apart: 5, of which 3 were waited for; matrix products, arithmetic and copies ran while one was open for 52% of the time, Pallas kernels for 0%

commit v1 on v0

v1 whole, which is shorter than its diff:
```python
import jax
import jax.numpy as jnp
from jax import lax
from jax.experimental import pallas as pl
from jax.experimental.pallas import tpu as pltpu
from jax.sharding import PartitionSpec as P

F32 = jnp.float32
BF16 = jnp.bfloat16


def pair_kernel(kmap_ref, count_ref, own_ref, incoming_ref, upstream_ref, weights_ref,
                out_ref, ghost_ref, own_grad_ref, wgrad_ref,
                pool, out_acc, pool_acc, weights, sems):
    taps = weights.shape[0]
    slots = kmap_ref.shape[0] // (2 * taps)
    own_total = own_ref.shape[0]
    pool_total = pool.shape[0] - 1
    copies = [
        pltpu.make_async_copy(own_ref, pool.at[pl.ds(0, own_total)], sems.at[0]),
        pltpu.make_async_copy(incoming_ref, pool.at[pl.ds(own_total, pool_total - own_total)], sems.at[1]),
        pltpu.make_async_copy(weights_ref, weights, sems.at[2]),
    ]
    for copy in copies:
        copy.start()
    pool[pool_total] = jnp.zeros(pool.shape[1:], BF16)
    out_acc[...] = jnp.zeros_like(out_acc)
    pool_acc[...] = jnp.zeros_like(pool_acc)
    for copy in copies:
        copy.wait()

    def tap_step(t, carry):
        count = count_ref[t]
        sources, targets = [], []
        for s in range(slots):
            live = s < count
            sources.append(jnp.where(live, kmap_ref[t * 2 * slots + s], pool_total))
            targets.append(jnp.where(live, kmap_ref[t * 2 * slots + slots + s], own_total))
        inputs = jnp.concatenate([pool[i] for i in sources], axis=0)
        upstream = jnp.concatenate(
            [upstream_ref[jnp.minimum(o, own_total - 1)] for o in targets], axis=0)
        tap = weights[t]
        forward = jnp.dot(inputs, tap, preferred_element_type=F32)
        backward = lax.dot_general(upstream, tap, (((1,), (1,)), ((), ())), preferred_element_type=F32)
        wgrad = lax.dot_general(inputs, upstream, (((0,), (0,)), ((), ())), preferred_element_type=F32)
        wgrad_ref[t] = wgrad.astype(BF16)
        rows = pool.shape[1]
        for s in range(slots):
            out_acc[targets[s]] += forward[s * rows:(s + 1) * rows]
            pool_acc[sources[s]] += backward[s * rows:(s + 1) * rows]
        return carry

    lax.fori_loop(0, taps, tap_step, 0)
    out_ref[...] = out_acc[:own_total].astype(BF16)
    own_grad_ref[...] = pool_acc[:own_total]
    ghost_ref[...] = pool_acc[own_total:pool_total].astype(BF16)


def pair_products(kmap, counts, own, incoming, upstream, weights):
    own_total, rows, channels = own.shape
    ghost_total = incoming.shape[0]
    taps = weights.shape[0]
    pool_total = own_total + ghost_total
    smem = pl.BlockSpec(memory_space=pltpu.SMEM)
    vmem = pl.BlockSpec(memory_space=pltpu.VMEM)
    hbm = pl.BlockSpec(memory_space=pl.ANY)
    flops = 3 * 2 * kmap.size // 2 * rows * channels * channels
    return pl.pallas_call(
        pair_kernel,
        out_shape=(
            jax.ShapeDtypeStruct((own_total, rows, channels), BF16),
            jax.ShapeDtypeStruct((ghost_total, rows, channels), BF16),
            jax.ShapeDtypeStruct((own_total, rows, channels), F32),
            jax.ShapeDtypeStruct((taps, channels, channels), BF16),
        ),
        in_specs=[smem, smem, hbm, hbm, vmem, hbm],
        out_specs=(vmem, vmem, vmem, vmem),
        scratch_shapes=[
            pltpu.VMEM((pool_total + 1, rows, channels), BF16),
            pltpu.VMEM((own_total + 1, rows, channels), F32),
            pltpu.VMEM((pool_total + 1, rows, channels), F32),
            pltpu.VMEM((taps, channels, channels), BF16),
            pltpu.SemaphoreType.DMA((3,)),
        ],
        cost_estimate=pl.CostEstimate(flops=flops, bytes_accessed=16 * 2 ** 20, transcendentals=0),
        compiler_params=pltpu.CompilerParams(vmem_limit_bytes=58 * 2 ** 20),
        name="pair_products",
    )(kmap.reshape(-1), counts, own, incoming, upstream, weights)


def on_device(feats, grad_out, kernel, send_bricks, kmap, pair_count):
    own = feats[0, 0]
    senders = send_bricks[0, 0]
    peers, cap = senders.shape
    own_total, rows, channels = own.shape
    taps, depth, _ = kernel.shape
    filled = senders >= 0
    outgoing = own[jnp.maximum(senders, 0)] * filled[:, :, None, None].astype(BF16)
    incoming = lax.all_to_all(outgoing, "dp", split_axis=0, concat_axis=0, tiled=True)
    weights = lax.all_gather(kernel, "fsdp", axis=1, tiled=True)
    produced, ghosts, own_grad, wgrad = pair_products(
        kmap[0, 0], pair_count[0, 0], own, incoming.reshape(peers * cap, rows, channels),
        grad_out[0, 0], weights)
    returned = lax.all_to_all(
        ghosts.reshape(peers, cap, rows, channels), "dp", split_axis=0, concat_axis=0, tiled=True)
    chosen = (senders.reshape(1, -1) == jnp.arange(own_total)[:, None]).astype(BF16)
    back = jnp.einsum("bk,kvc->bvc", chosen, returned.reshape(peers * cap, rows, channels),
                      preferred_element_type=F32)
    in_grad = (own_grad + back).astype(BF16)
    divisor = F32(4 * lax.axis_size("dp") * lax.axis_size("fsdp"))
    portion = lax.psum_scatter(wgrad, "fsdp", scatter_dimension=1, tiled=True)
    portion = portion.reshape(taps * depth, channels)
    share = -(-taps * depth // (16 * peers)) * 16
    portion = jnp.pad(portion, ((0, share * peers - taps * depth), (0, 0)))
    pieces = lax.all_to_all(portion.reshape(peers, share, channels), "dp", 0, 0, tiled=True)
    total = jnp.sum(pieces.astype(F32), axis=0).astype(BF16)
    whole = lax.all_gather(total, "dp", axis=0, tiled=True)[:taps * depth]
    kernel_grad = whole.reshape(taps, depth, channels).astype(F32) / divisor
    return (produced[None, None], in_grad[None, None], kernel_grad)


def solution(mesh):
    bricks = P("dp", "fsdp", None, None, None)
    return jax.shard_map(
        on_device,
        mesh=mesh,
        in_specs=(bricks, bricks, P(None, "fsdp", None), P("dp", "fsdp", None, None),
                  P("dp", "fsdp", None, None, None), P("dp", "fsdp", None)),
        out_specs=(bricks, bricks, P(None, "fsdp", None)),
        check_vma=False,
    )
```

time: 239 us -> 174 us (0.73)
  the two profiles are of different devices: /device:TPU:12 before, /device:TPU:0 now
where the time goes in v1:
time: 174 us; the launch traced here: 173 us
  waiting for transfers between devices  82.7 us (48%)
  blocking collectives  32.6 us (19%)
  starting transfers between devices  16.6 us (10%)
  Pallas kernels  15.8 us (9%)
  between operations  14.1 us (8%)
  local copies, waits for them, and re-layouts  6.03 us (3%)
  other arithmetic  5.05 us (3%)
    reduce_scatter x1, waiting for transfers between devices, on_device(): portion = lax.psum_scatter(wgrad, 'fsdp', scatter_dimension=1, tiled=True)  36 us
    all_gather x1, blocking collectives, on_device(): whole = lax.all_gather(total, 'dp', axis=0, tiled=True)[:taps * depth]  32.6 us
    all_to_all x1, waiting for transfers between devices, on_device(): lax.all_to_all(outgoing, 'dp', split_axis=0, concat_axis=0, tiled=True)  24.9 us
    all_to_all x1, waiting for transfers between devices, on_device(): lax.all_to_all(portion.reshape(peers, share, channels), 'dp', 0, 0, tiled...  21.1 us
    pallas_call x1, Pallas kernels, pair_products(): pl.pallas_call(pair_kernel, out_shape=(jax.ShapeDtypeStruct((own_total, r...  15.8 us
    all_to_all x1, starting transfers between devices, on_device(): lax.all_to_all(outgoing, 'dp', split_axis=0, concat_axis=0, tiled=True)  7.28 us
    all_to_all x1, starting transfers between devices, on_device(): lax.all_to_all(portion.reshape(peers, share, channels), 'dp', 0, 0, tiled...  5.63 us
    all_to_all x1, starting transfers between devices, on_device(): lax.all_to_all(ghosts.reshape(peers, cap, rows, channels), 'dp', split_ax...  3.6 us
  transfers between devices with their start and end apart: 5, of which 3 were waited for; matrix products, arithmetic and copies ran while one was open for 5% of the time, Pallas kernels for 0%

profile of v1, /device:TPU:0, one launch (start us, length us, event | category | flops | bytes accessed | tf_op | source)
XLA Modules:
  0.0 173.4 jit_solution(14336407264066410455)
XLA Ops:
  7.2 0.7 all-gather.2.cloned.1.call-update
  7.9 0.7 broadcast_maximum_fusion
  8.6 0.1 copy.15
  8.7 0.1 reshape.57
  8.7 0.7 fusion.7
  9.4 0.1 copy.16
  9.5 1.7 gather_fusion
  11.2 1.1 broadcast_multiply_fusion
  12.3 7.3 %all-to-all-start = ((bf16[8,2,128,256]{3,2,1,0:T(8,128)(2,1)}), bf16[8,2,128,256]{3,2,1,0:T(8,128)(2,1)S(1)}, u32[]{:S(2)}, u32[]{:S(2)}) async-start(bf16[8,2,128,256]{3,2,1,0:T(8,128)(2,1)} %broadcast_multiply_fusion), calls=%async_computation | async-start | bytes 2097152 | tf_op jit(solution)/shard_map/all_to_all | solution.py:99
  19.7 0.1 copy.14
  19.8 0.7 reshape_squeeze.4.kmap_ref
  20.5 24.9 %all-to-all-done = bf16[8,2,128,256]{3,2,1,0:T(8,128)(2,1)S(1)} async-done(((bf16[8,2,128,256]{3,2,1,0:T(8,128)(2,1)}), bf16[8,2,128,256]{3,2,1,0:T(8,128)(2,1)S(1)}, u32[]{:S(2)}, u32[]{:S(2)}) %all-to-all-start) | async-done | bytes 1048608 | tf_op jit(solution)/shard_map/all_to_all | solution.py:99
  45.4 1.0 copy-done.1
  46.3 15.8 %pair_products.1 = (bf16[8,128,256]{2,1,0:T(8,128)(2,1)}, bf16[16,128,256]{2,1,0:T(8,128)(2,1)}, f32[8,128,256]{2,1,0:T(8,128)}, bf16[27,256,256]{2,1,0:T(8,128)(2,1)}) custom-call(s32[162]{0:T(256)} %reshape_squeeze.4.kmap_ref, s32[27]{0:T(128)} %bitcast.30, bf16[8,128,256]{2,1,0:T(8,128)(2,1)} %bitcast.25, bf16[16,128,256]{2,1,0:T(8,128)(2,1)} %bitcast.27, ...), custom_call_target="tpu_custom_call" | custom-call | flops 4076863488 | bytes 16777216 | tf_op jit(solution)/shard_map/pair_products/pallas_call | solution.py:68
  62.1 3.6 %all-to-all-start.1 = ((bf16[8,2,128,256]{3,2,1,0:T(8,128)(2,1)}), bf16[8,2,128,256]{3,2,1,0:T(8,128)(2,1)S(1)}, u32[]{:S(2)}, u32[]{:S(2)}) async-start(bf16[8,2,128,256]{3,2,1,0:T(8,128)(2,1)} %bitcast.8), calls=%async_computation.1 | async-start | bytes 2097152 | tf_op jit(solution)/shard_map/all_to_all | solution.py:104
  65.7 36.0 %reduce-scatter.2.cloned.1.call-done = bf16[27,64,256]{2,1,0:T(8,128)(2,1)} async-done(((bf16[27,256,256]{2,1,0:T(8,128)(2,1)}), bf16[27,64,256]{2,1,0:T(8,128)(2,1)}) %reduce-scatter.2.cloned.1.call-update) | async-done | bytes 884752 | tf_op jit(solution)/shard_map/reduce_scatter | solution.py:111
  101.7 2.2 %pad.4 = bf16[1792,256]{1,0:T(8,128)(2,1)} pad(bf16[1728,256]{1,0:T(8,128)(2,1)} %bitcast.28, bf16[]{:T(256)} %constant.10.clone.1), padding=0_64x0_0 | pad | bytes 1802242 | tf_op jit(solution)/shard_map/jit(_pad)/pad | solution.py:114
  103.9 5.6 %all-to-all-start.2 = ((bf16[8,224,256]{2,1,0:T(8,128)(2,1)}), bf16[8,224,256]{2,1,0:T(8,128)(2,1)S(1)}, u32[]{:S(2)}, u32[]{:S(2)}) async-start(bf16[8,224,256]{2,1,0:T(8,128)(2,1)} %bitcast.12), calls=%async_computation.3 | async-start | bytes 1835008 | tf_op jit(solution)/shard_map/all_to_all | solution.py:115
  109.7 0.7 fusion
  110.4 1.1 fusion.3
  111.5 21.1 %all-to-all-done.2 = bf16[8,224,256]{2,1,0:T(8,128)(2,1)S(1)} async-done(((bf16[8,224,256]{2,1,0:T(8,128)(2,1)}), bf16[8,224,256]{2,1,0:T(8,128)(2,1)S(1)}, u32[]{:S(2)}, u32[]{:S(2)}) %all-to-all-start.2) | async-done | bytes 917536 | tf_op jit(solution)/shard_map/all_to_all | solution.py:115
  132.6 0.1 reduce_sum.12
  132.7 32.6 %all_gather.7 = bf16[1792,256]{1,0:T(8,128)(2,1)S(1)} all-gather(bf16[224,256]{1,0:T(8,128)(2,1)S(1)} %reduce_sum.12), channel_id=1, replica_groups=mesh['dp'=8,'fsdp'=4] {'dp'}, dimensions={0}, use_global_device_ids=true | all-gather | bytes 1032192 | tf_op jit(solution)/shard_map/all_gather | solution.py:117
  165.3 1.3 convert_multiply_fusion
  (15 shorter events, 0.3 us)
Async XLA Ops:
  7.2 38.2 %all-gather.2.cloned.1.call-start = ((), (), s32[]{:S(2)}) async-start(), calls=%async_computation.4 | async-start | bytes 4423680 | tf_op jit(solution)/shard_map/all_gather | solution.py:100
  11.2 8.5 %copy-start.3 = (s32[1,1,27,2,3]{2,3,4,1,0:T(2,128)S(1)}, s32[1,1,27,2,3]{2,3,4,1,0:T(2,128)}, u32[]{:S(2)}) copy-start(s32[1,1,27,2,3]{2,3,4,1,0:T(2,128)} %param.10) | copy-start | bytes 1948
  12.3 33.0 %all-to-all-start = ((bf16[8,2,128,256]{3,2,1,0:T(8,128)(2,1)}), bf16[8,2,128,256]{3,2,1,0:T(8,128)(2,1)S(1)}, u32[]{:S(2)}, u32[]{:S(2)}) async-start(bf16[8,2,128,256]{3,2,1,0:T(8,128)(2,1)} %broadcast_multiply_fusion), calls=%async_computation | async-start | bytes 2097152 | tf_op jit(solution)/shard_map/all_to_all | solution.py:99
  19.6 82.1 %reduce-scatter.2.cloned.1.call-start = ((), (), s32[]{:S(2)}) async-start(), calls=%async_computation.5 | async-start | bytes 4423680 | tf_op jit(solution)/shard_map/reduce_scatter | solution.py:111
  45.4 1.0 copy-start.1
  62.1 41.8 %all-to-all-start.1 = ((bf16[8,2,128,256]{3,2,1,0:T(8,128)(2,1)}), bf16[8,2,128,256]{3,2,1,0:T(8,128)(2,1)S(1)}, u32[]{:S(2)}, u32[]{:S(2)}) async-start(bf16[8,2,128,256]{3,2,1,0:T(8,128)(2,1)} %bitcast.8), calls=%async_computation.1 | async-start | bytes 2097152 | tf_op jit(solution)/shard_map/all_to_all | solution.py:104
  101.7 7.8 %copy-start.2 = (s32[1,1,8,2]{2,3,1,0:T(2,128)S(1)}, s32[1,1,8,2]{2,3,1,0:T(2,128)}, u32[]{:S(2)}) copy-start(s32[1,1,8,2]{2,3,1,0:T(2,128)} %param.9) | copy-start | bytes 196
  103.9 6.5 %copy-start = (f32[8,128,256]{2,1,0:T(8,128)S(1)}, f32[8,128,256]{2,1,0:T(8,128)}, u32[]{:S(2)}) copy-start(f32[8,128,256]{2,1,0:T(8,128)} %get-tuple-element.8) | copy-start | bytes 3145732
  103.9 28.7 %all-to-all-start.2 = ((bf16[8,224,256]{2,1,0:T(8,128)(2,1)}), bf16[8,224,256]{2,1,0:T(8,128)(2,1)S(1)}, u32[]{:S(2)}, u32[]{:S(2)}) async-start(bf16[8,224,256]{2,1,0:T(8,128)(2,1)} %bitcast.12), calls=%async_computation.3 | async-start | bytes 1835008 | tf_op jit(solution)/shard_map/all_to_all | solution.py:115
Sparse Core Ops, SparseCore 0:
  9.6 33.4 all-gather.1
  62.3 39.4 reduce-scatter.1

commit v2 on v1

--- a/solution.py
+++ b/solution.py
@@ -88,6 +88,157 @@
     )(kmap.reshape(-1), counts, own, incoming, upstream, weights)
 
 
+def reduce_kernel(wgrad_ref, ghost_ref, whole_ref, returned_ref,
+                  near, far, crossed, portion, pieces, acc, total,
+                  near_sems, far_sems, piece_sems, whole_sems, ghost_sems, local_sems):
+    peers = lax.axis_size("dp")
+    me = lax.axis_index("dp")
+    column = lax.axis_index("fsdp")
+    sibling = column + 1 - 2 * lax.rem(column, 2)
+    across = column + 2 - 4 * lax.rem(lax.div(column, 2), 2)
+    diagonal = sibling + 2 - 4 * lax.rem(lax.div(sibling, 2), 2)
+    taps, depth, _ = far.shape
+    share = total.shape[0]
+    cap = ghost_ref.shape[0] // peers
+
+    def peer_of(step):
+        return lax.rem(me + step, peers)
+
+    barrier = pltpu.get_barrier_semaphore()
+
+    def greet(step, carry):
+        pl.semaphore_signal(barrier, inc=1, device_id=(peer_of(step), column),
+                            device_id_type=pl.DeviceIdType.MESH)
+        return carry
+
+    for other in (sibling, across):
+        pl.semaphore_signal(barrier, inc=1, device_id=(me, other),
+                            device_id_type=pl.DeviceIdType.MESH)
+    lax.fori_loop(1, peers, greet, 0)
+    pl.semaphore_wait(barrier, peers + 1)
+
+    def remote(source, target, sems, step, device):
+        return pltpu.make_async_remote_copy(
+            src_ref=source, dst_ref=target, send_sem=sems.at[0, step], recv_sem=sems.at[1, step],
+            device_id=device, device_id_type=pl.DeviceIdType.MESH)
+
+    def shard(index):
+        return wgrad_ref.at[:, pl.ds(pl.multiple_of(index * depth, depth), depth), :]
+
+    to_far = remote(shard(diagonal), near.at[1], near_sems, 1, (me, sibling))
+    to_near = remote(shard(sibling), near.at[0], near_sems, 0, (me, sibling))
+    to_far.start()
+    to_near.start()
+
+    def ghost_copy(step):
+        peer = peer_of(step)
+        return remote(ghost_ref.at[pl.ds(peer * cap, cap)], returned_ref.at[pl.ds(me * cap, cap)],
+                      ghost_sems, step, (peer, column))
+
+    def piece_copy(step):
+        peer = peer_of(step)
+        return remote(portion.at[pl.ds(pl.multiple_of(peer * share, 16), share)], pieces.at[step],
+                      piece_sems, step, (peer, column))
+
+    def whole_copy(step):
+        return remote(total, whole_ref.at[pl.ds(pl.multiple_of(me * share, 16), share)],
+                      whole_sems, step, (peer_of(step), column))
+
+    def begin(copy):
+        def go(step, carry):
+            copy(step).start()
+            return carry
+        lax.fori_loop(1, peers, go, 0)
+
+    def finish(copy):
+        def go(step, carry):
+            copy(step).wait()
+            return carry
+        lax.fori_loop(1, peers, go, 0)
+
+    begin(ghost_copy)
+    kept = pltpu.make_async_copy(ghost_ref.at[pl.ds(me * cap, cap)],
+                                 returned_ref.at[pl.ds(me * cap, cap)], local_sems.at[0])
+    kept.start()
+
+    def load(index, t):
+        return wgrad_ref[t, pl.ds(pl.multiple_of(index * depth, depth), depth), :].astype(F32)
+
+    to_far.wait()
+
+    def far_sum(t, carry):
+        far[t] = (load(across, t) + near[1, t].astype(F32)).astype(BF16)
+        return carry
+
+    lax.fori_loop(0, taps, far_sum, 0)
+    to_across = remote(far, crossed, far_sems, 0, (me, across))
+    to_across.start()
+    padding = portion.shape[0] - taps * depth
+    if padding:
+        portion[pl.ds(taps * depth, padding), :] = jnp.zeros((padding, portion.shape[1]), BF16)
+    to_near.wait()
+    to_across.wait()
+
+    def near_sum(t, carry):
+        value = load(column, t) + near[0, t].astype(F32) + crossed[t].astype(F32)
+        portion[pl.ds(pl.multiple_of(t * depth, depth), depth), :] = value.astype(BF16)
+        return carry
+
+    lax.fori_loop(0, taps, near_sum, 0)
+    begin(piece_copy)
+    acc[...] = portion[pl.ds(pl.multiple_of(me * share, 16), share), :].astype(F32)
+
+    def add_piece(step, carry):
+        piece_copy(step).wait()
+        acc[...] += pieces[step].astype(F32)
+        return carry
+
+    lax.fori_loop(1, peers, add_piece, 0)
+    total[...] = acc[...].astype(BF16)
+    begin(whole_copy)
+    mine = pltpu.make_async_copy(
+        total, whole_ref.at[pl.ds(pl.multiple_of(me * share, 16), share)], local_sems.at[1])
+    mine.start()
+    mine.wait()
+    kept.wait()
+    finish(ghost_copy)
+    finish(whole_copy)
+
+
+def reduce_and_return(wgrad, ghosts, peers, depth):
+    taps, _, channels = wgrad.shape
+    share = -(-taps * depth // (16 * peers)) * 16
+    vmem = pl.BlockSpec(memory_space=pltpu.VMEM)
+    hbm = pl.BlockSpec(memory_space=pl.ANY)
+    return pl.pallas_call(
+        reduce_kernel,
+        out_shape=(
+            jax.ShapeDtypeStruct((share * peers, channels), BF16),
+            jax.ShapeDtypeStruct(ghosts.shape, BF16),
+        ),
+        in_specs=[vmem, hbm],
+        out_specs=(hbm, hbm),
+        scratch_shapes=[
+            pltpu.VMEM((2, taps, depth, channels), BF16),
+            pltpu.VMEM((taps, depth, channels), BF16),
+            pltpu.VMEM((taps, depth, channels), BF16),
+            pltpu.VMEM((share * peers, channels), BF16),
+            pltpu.VMEM((peers, share, channels), BF16),
+            pltpu.VMEM((share, channels), F32),
+            pltpu.VMEM((share, channels), BF16),
+            pltpu.SemaphoreType.DMA((2, 2)),
+            pltpu.SemaphoreType.DMA((2, 1)),
+            pltpu.SemaphoreType.DMA((2, peers)),
+            pltpu.SemaphoreType.DMA((2, peers)),
+            pltpu.SemaphoreType.DMA((2, peers)),
+            pltpu.SemaphoreType.DMA((2,)),
+        ],
+        compiler_params=pltpu.CompilerParams(
+            collective_id=0, has_side_effects=True, vmem_limit_bytes=40 * 2 ** 20),
+        name="reduce_and_return",
+    )(wgrad, ghosts)
+
+
 def on_device(feats, grad_out, kernel, send_bricks, kmap, pair_count):
     own = feats[0, 0]
     senders = send_bricks[0, 0]
@@ -101,21 +252,13 @@
     produced, ghosts, own_grad, wgrad = pair_products(
         kmap[0, 0], pair_count[0, 0], own, incoming.reshape(peers * cap, rows, channels),
         grad_out[0, 0], weights)
-    returned = lax.all_to_all(
-        ghosts.reshape(peers, cap, rows, channels), "dp", split_axis=0, concat_axis=0, tiled=True)
+    whole, returned = reduce_and_return(wgrad, ghosts, peers, depth)
     chosen = (senders.reshape(1, -1) == jnp.arange(own_total)[:, None]).astype(BF16)
-    back = jnp.einsum("bk,kvc->bvc", chosen, returned.reshape(peers * cap, rows, channels),
+    back = jnp.einsum("bk,kvc->bvc", chosen, returned,
                       preferred_element_type=F32)
     in_grad = (own_grad + back).astype(BF16)
     divisor = F32(4 * lax.axis_size("dp") * lax.axis_size("fsdp"))
-    portion = lax.psum_scatter(wgrad, "fsdp", scatter_dimension=1, tiled=True)
-    portion = portion.reshape(taps * depth, channels)
-    share = -(-taps * depth // (16 * peers)) * 16
-    portion = jnp.pad(portion, ((0, share * peers - taps * depth), (0, 0)))
-    pieces = lax.all_to_all(portion.reshape(peers, share, channels), "dp", 0, 0, tiled=True)
-    total = jnp.sum(pieces.astype(F32), axis=0).astype(BF16)
-    whole = lax.all_gather(total, "dp", axis=0, tiled=True)[:taps * depth]
-    kernel_grad = whole.reshape(taps, depth, channels).astype(F32) / divisor
+    kernel_grad = whole[:taps * depth].reshape(taps, depth, channels).astype(F32) / divisor
     return (produced[None, None], in_grad[None, None], kernel_grad)
 
 

time: 174 us -> 142 us (0.82)
  the two profiles are of different devices: /device:TPU:0 before, /device:TPU:12 now
where the time goes in v2:
time: 142 us
  Pallas kernels  86.5 us (61%)
  waiting for transfers between devices  22.6 us (16%)
  between operations  14.1 us (10%)
  local copies, waits for them, and re-layouts  6.63 us (5%)
  starting transfers between devices  6.26 us (4%)
  other arithmetic  4.92 us (3%)
    pallas_call x1, Pallas kernels, reduce_and_return(): pl.pallas_call(reduce_kernel, out_shape=(jax.ShapeDtypeStruct((share * pe...  70.7 us
    all_to_all x1, waiting for transfers between devices, on_device(): lax.all_to_all(outgoing, 'dp', split_axis=0, concat_axis=0, tiled=True)  21.5 us
    pallas_call x1, Pallas kernels, pair_products(): pl.pallas_call(pair_kernel, out_shape=(jax.ShapeDtypeStruct((own_total, r...  15.8 us
    all_to_all x1, starting transfers between devices, on_device(): lax.all_to_all(outgoing, 'dp', split_axis=0, concat_axis=0, tiled=True)  6.22 us
    unnamed x14, local copies, waits for them, and re-layouts  3.93 us
  transfers between devices with their start and end apart: 2, of which 2 were waited for; matrix products, arithmetic and copies ran while one was open for 4% of the time, Pallas kernels for 0%

profile of v2, /device:TPU:12, one launch (start us, length us, event | category | flops | bytes accessed | tf_op | source)
XLA Modules:
  0.0 141.6 jit_solution(11307517228476148842)
XLA Ops:
  7.2 0.0 all-gather.2.cloned.1.call-start
  7.2 0.7 all-gather.2.cloned.1.call-update
  7.9 0.7 broadcast_maximum_fusion
  8.6 0.1 copy.15
  8.7 0.1 reshape.41
  8.7 0.7 fusion.7
  9.4 0.1 copy.16
  9.5 1.7 %gather_fusion = bf16[16,128,256]{2,1,0:T(8,128)(2,1)S(1)} fusion(bf16[8,128,256]{2,1,0:T(8,128)(2,1)} %bitcast.19, s32[1024]{0:T(1024)S(1)} %pad_clamp_fusion), kind=kCustom, calls=%fused_computation | custom fusion | bytes 2097216 | tf_op jit(solution)/shard_map/gather | solution.py:249
  11.2 1.1 broadcast_multiply_fusion
  12.3 6.2 %all-to-all-start = ((bf16[8,2,128,256]{3,2,1,0:T(8,128)(2,1)}), bf16[8,2,128,256]{3,2,1,0:T(8,128)(2,1)S(1)}, u32[]{:S(2)}, u32[]{:S(2)}) async-start(bf16[8,2,128,256]{3,2,1,0:T(8,128)(2,1)} %broadcast_multiply_fusion), calls=%async_computation | async-start | bytes 2097152 | tf_op jit(solution)/shard_map/all_to_all | solution.py:250
  18.6 0.1 copy.17
  18.6 0.1 copy.14
  18.8 0.7 reshape_squeeze.4.kmap_ref
  19.5 0.1 eq.15
  19.5 21.5 %all-to-all-done = bf16[8,2,128,256]{3,2,1,0:T(8,128)(2,1)S(1)} async-done(((bf16[8,2,128,256]{3,2,1,0:T(8,128)(2,1)}), bf16[8,2,128,256]{3,2,1,0:T(8,128)(2,1)S(1)}, u32[]{:S(2)}, u32[]{:S(2)}) %all-to-all-start) | async-done | bytes 1048608 | tf_op jit(solution)/shard_map/all_to_all | solution.py:250
  41.0 0.5 all-gather.2.cloned.1.call-done.weights_ref
  41.5 0.5 copy-done.2
  42.0 15.8 %pair_products.1 = (bf16[8,128,256]{2,1,0:T(8,128)(2,1)}, bf16[16,128,256]{2,1,0:T(8,128)(2,1)}, f32[8,128,256]{2,1,0:T(8,128)}, bf16[27,256,256]{2,1,0:T(8,128)(2,1)}) custom-call(s32[162]{0:T(256)} %reshape_squeeze.4.kmap_ref, s32[27]{0:T(128)} %bitcast.24, bf16[8,128,256]{2,1,0:T(8,128)(2,1)} %bitcast.20, bf16[16,128,256]{2,1,0:T(8,128)(2,1)} %bitcast.22, ...), custom_call_target="tpu_custom_call" | custom-call | flops 4076863488 | bytes 16777216 | tf_op jit(solution)/shard_map/pair_products/pallas_call | solution.py:68
  57.8 2.0 %copy-done = bf16[27,256,256]{2,1,0:T(8,128)(2,1)S(1)} copy-done((bf16[27,256,256]{2,1,0:T(8,128)(2,1)S(1)}, bf16[27,256,256]{2,1,0:T(8,128)(2,1)}, u32[]{:S(2)}) %copy-start) | copy-done | bytes 3538968
  59.7 1.2 copy-done.1
  61.0 70.7 %reduce_and_return.1 = (bf16[1792,256]{1,0:T(8,128)(2,1)S(1)}, bf16[16,128,256]{2,1,0:T(8,128)(2,1)S(1)}) custom-call(bf16[27,256,256]{2,1,0:T(8,128)(2,1)S(1)} %copy-done, bf16[16,128,256]{2,1,0:T(8,128)(2,1)S(1)} %copy-done.1), custom_call_target="tpu_custom_call" | custom-call | tf_op jit(solution)/shard_map/reduce_and_return/pallas_call | solution.py:213
  131.7 1.3 convert_multiply_fusion
  133.0 0.7 fusion.1
  133.7 1.1 fusion.3
  (10 shorter events, 0.0 us)
Async XLA Ops:
  7.2 34.3 %all-gather.2.cloned.1.call-start = ((), (), s32[]{:S(2)}) async-start(), calls=%async_computation.1 | async-start | bytes 4423680 | tf_op jit(solution)/shard_map/all_gather | solution.py:251
  11.2 7.4 %copy-start.4 = (s32[1,1,8,2]{2,3,1,0:T(2,128)S(1)}, s32[1,1,8,2]{2,3,1,0:T(2,128)}, u32[]{:S(2)}) copy-start(s32[1,1,8,2]{2,3,1,0:T(2,128)} %param.9) | copy-start | bytes 196
  11.2 7.4 %copy-start.5 = (s32[1,1,27,2,3]{2,3,4,1,0:T(2,128)S(1)}, s32[1,1,27,2,3]{2,3,4,1,0:T(2,128)}, u32[]{:S(2)}) copy-start(s32[1,1,27,2,3]{2,3,4,1,0:T(2,128)} %param.10) | copy-start | bytes 1948
  12.3 28.7 %all-to-all-start = ((bf16[8,2,128,256]{3,2,1,0:T(8,128)(2,1)}), bf16[8,2,128,256]{3,2,1,0:T(8,128)(2,1)S(1)}, u32[]{:S(2)}, u32[]{:S(2)}) async-start(bf16[8,2,128,256]{3,2,1,0:T(8,128)(2,1)} %broadcast_multiply_fusion), calls=%async_computation | async-start | bytes 2097152 | tf_op jit(solution)/shard_map/all_to_all | solution.py:250
  41.0 1.0 copy-start.2
  57.7 2.0 %copy-start = (bf16[27,256,256]{2,1,0:T(8,128)(2,1)S(1)}, bf16[27,256,256]{2,1,0:T(8,128)(2,1)}, u32[]{:S(2)}) copy-start(bf16[27,256,256]{2,1,0:T(8,128)(2,1)} %get-tuple-element.11.wgrad_ref) | copy-start | bytes 10616836
  59.7 1.2 copy-start.1
  131.7 2.0 %copy-start.3 = (f32[8,128,256]{2,1,0:T(8,128)S(1)}, f32[8,128,256]{2,1,0:T(8,128)}, u32[]{:S(2)}) copy-start(f32[8,128,256]{2,1,0:T(8,128)} %get-tuple-element.10) | copy-start | bytes 3145732
Sparse Core Ops, SparseCore 0:
  9.6 31.8 all-gather.1

commit v3 on v2

--- a/solution.py
+++ b/solution.py
@@ -239,18 +239,119 @@
     )(wgrad, ghosts)
 
 
+def gather_kernel(senders_ref, own_ref, kernel_ref, incoming_ref, weights_ref,
+                  outgoing, weight_sems, brick_sems, local_sems):
+    peers = lax.axis_size("dp")
+    me = lax.axis_index("dp")
+    column = lax.axis_index("fsdp")
+    sibling = column + 1 - 2 * lax.rem(column, 2)
+    across = column + 2 - 4 * lax.rem(lax.div(column, 2), 2)
+    depth = kernel_ref.shape[1]
+    cap = outgoing.shape[0] // peers
+
+    def peer_of(step):
+        return lax.rem(me + step, peers)
+
+    barrier = pltpu.get_barrier_semaphore()
+
+    def greet(step, carry):
+        pl.semaphore_signal(barrier, inc=1, device_id=(peer_of(step), column),
+                            device_id_type=pl.DeviceIdType.MESH)
+        return carry
+
+    for other in (sibling, across):
+        pl.semaphore_signal(barrier, inc=1, device_id=(me, other),
+                            device_id_type=pl.DeviceIdType.MESH)
+    lax.fori_loop(1, peers, greet, 0)
+    pl.semaphore_wait(barrier, peers + 1)
+
+    def shard(index):
+        return weights_ref.at[:, pl.ds(pl.multiple_of(index * depth, depth), depth), :]
+
+    def remote(source, target, sems, step, device):
+        return pltpu.make_async_remote_copy(
+            src_ref=source, dst_ref=target, send_sem=sems.at[0, step], recv_sem=sems.at[1, step],
+            device_id=device, device_id_type=pl.DeviceIdType.MESH)
+
+    to_across = remote(kernel_ref, shard(column), weight_sems, 0, (me, across))
+    to_sibling = remote(kernel_ref, shard(column), weight_sems, 1, (me, sibling))
+    to_across.start()
+    to_sibling.start()
+    kept = pltpu.make_async_copy(kernel_ref, shard(column), local_sems.at[0])
+    kept.start()
+
+    def fill(peer):
+        for c in range(cap):
+            brick = senders_ref[peer * cap + c]
+            mask = (brick >= 0).astype(F32)
+            value = own_ref[jnp.maximum(brick, 0)].astype(F32) * mask
+            outgoing[peer * cap + c] = value.astype(BF16)
+
+    def brick_copy(step):
+        peer = peer_of(step)
+        return remote(outgoing.at[pl.ds(peer * cap, cap)], incoming_ref.at[pl.ds(me * cap, cap)],
+                      brick_sems, step, (peer, column))
+
+    def send(step, carry):
+        fill(peer_of(step))
+        brick_copy(step).start()
+        return carry
+
+    lax.fori_loop(1, peers, send, 0)
+    fill(me)
+    mine = pltpu.make_async_copy(outgoing.at[pl.ds(me * cap, cap)],
+                                 incoming_ref.at[pl.ds(me * cap, cap)], local_sems.at[1])
+    mine.start()
+    to_across.wait()
+    forward = remote(shard(across), shard(across), weight_sems, 2, (me, sibling))
+    forward.start()
+    to_sibling.wait()
+    kept.wait()
+    mine.wait()
+
+    def finish(step, carry):
+        brick_copy(step).wait()
+        return carry
+
+    lax.fori_loop(1, peers, finish, 0)
+    forward.wait()
+
+
+def gather_inputs(senders, own, kernel, columns):
+    peers, cap = senders.shape
+    taps, depth, channels = kernel.shape
+    bricks = (peers * cap,) + own.shape[1:]
+    hbm = pl.BlockSpec(memory_space=pl.ANY)
+    return pl.pallas_call(
+        gather_kernel,
+        out_shape=(
+            jax.ShapeDtypeStruct(bricks, BF16),
+            jax.ShapeDtypeStruct((taps, depth * columns, channels), BF16),
+        ),
+        in_specs=[pl.BlockSpec(memory_space=pltpu.SMEM),
+                  pl.BlockSpec(memory_space=pltpu.VMEM), hbm],
+        out_specs=(hbm, hbm),
+        scratch_shapes=[
+            pltpu.VMEM(bricks, BF16),
+            pltpu.SemaphoreType.DMA((2, 3)),
+            pltpu.SemaphoreType.DMA((2, peers)),
+            pltpu.SemaphoreType.DMA((2,)),
+        ],
+        compiler_params=pltpu.CompilerParams(
+            collective_id=1, has_side_effects=True, vmem_limit_bytes=40 * 2 ** 20),
+        name="gather_inputs",
+    )(senders.reshape(-1), own, kernel)
+
+
 def on_device(feats, grad_out, kernel, send_bricks, kmap, pair_count):
     own = feats[0, 0]
     senders = send_bricks[0, 0]
-    peers, cap = senders.shape
-    own_total, rows, channels = own.shape
+    peers = senders.shape[0]
+    own_total, _, channels = own.shape
     taps, depth, _ = kernel.shape
-    filled = senders >= 0
-    outgoing = own[jnp.maximum(senders, 0)] * filled[:, :, None, None].astype(BF16)
-    incoming = lax.all_to_all(outgoing, "dp", split_axis=0, concat_axis=0, tiled=True)
-    weights = lax.all_gather(kernel, "fsdp", axis=1, tiled=True)
+    incoming, weights = gather_inputs(senders, own, kernel, lax.axis_size("fsdp"))
     produced, ghosts, own_grad, wgrad = pair_products(
-        kmap[0, 0], pair_count[0, 0], own, incoming.reshape(peers * cap, rows, channels),
+        kmap[0, 0], pair_count[0, 0], own, incoming,
         grad_out[0, 0], weights)
     whole, returned = reduce_and_return(wgrad, ghosts, peers, depth)
     chosen = (senders.reshape(1, -1) == jnp.arange(own_total)[:, None]).astype(BF16)

time: 142 us -> 130 us (0.915)
  Pallas kernels: 86.5 us -> 114 us
  waiting for transfers between devices: 22.6 us -> 0 us
  between operations: 14.1 us -> 0.69 us
  starting transfers between devices: 6.26 us -> 0 us
  local copies, waits for them, and re-layouts: 6.63 us -> 11 us
  other arithmetic: 4.92 us -> 2.44 us
    pallas_call x0 -> x1, Pallas kernels: none -> 28 us  [gather_inputs(): pl.pallas_call(gather_kernel, out_shape=(jax.ShapeDtypeStruct(bricks, BF1...]
    all_to_all x1 -> x0, waiting for transfers between devices: 21.5 us -> none  [on_device(): lax.all_to_all(outgoing, 'dp', split_axis=0, concat_axis=0, tiled=True)]
    unnamed x14 -> x16, local copies, waits for them, and re-layouts: 3.93 us -> 10.2 us
    all_to_all x1 -> x0, starting transfers between devices: 6.22 us -> none  [on_device(): lax.all_to_all(outgoing, 'dp', split_axis=0, concat_axis=0, tiled=True)]
    gather x1 -> x0, local copies, waits for them, and re-layouts: 1.65 us -> none  [on_device(): own[jnp.maximum(senders, 0)] * filled[:, :, None, None].astype(BF16)]
  transfers between devices with their start and end apart: 2 -> 0, of which waited for: 2 -> 0; matrix products, arithmetic and copies ran while one was open for 4% -> 0% of each run, Pallas kernels for 0% -> 0%
where the time goes in v3:
time: 130 us; the launch traced here: 129 us
  Pallas kernels  114 us (88%)
  local copies, waits for them, and re-layouts  11 us (8%)
  other arithmetic  2.44 us (2%)
    pallas_call x1, Pallas kernels, reduce_and_return(): pl.pallas_call(reduce_kernel, out_shape=(jax.ShapeDtypeStruct((share * pe...  70.1 us
    pallas_call x1, Pallas kernels, gather_inputs(): pl.pallas_call(gather_kernel, out_shape=(jax.ShapeDtypeStruct(bricks, BF1...  28 us
    pallas_call x1, Pallas kernels, pair_products(): pl.pallas_call(pair_kernel, out_shape=(jax.ShapeDtypeStruct((own_total, r...  15.8 us
    unnamed x16, local copies, waits for them, and re-layouts  10.2 us

profile of v3, /device:TPU:12, one launch (start us, length us, event | category | flops | bytes accessed | tf_op | source)
XLA Modules:
  0.0 128.7 jit_solution(9743622644949188082)
XLA Ops:
  0.6 0.8 copy.13
  1.4 0.1 reshape_squeeze.8.senders_ref
  1.5 0.8 copy.12
  2.3 0.7 reshape_squeeze.7.kmap_ref
  3.0 0.0 copy-start.2
  3.0 1.2 copy-done.2
  4.1 0.0 copy-start.3
  4.1 1.0 copy-done.3
  5.2 28.0 %gather_inputs.1 = (bf16[16,128,256]{2,1,0:T(8,128)(2,1)S(1)}, bf16[27,256,256]{2,1,0:T(8,128)(2,1)S(1)}) custom-call(s32[16]{0:T(128)S(1)} %reshape_squeeze.8.senders_ref, bf16[8,128,256]{2,1,0:T(8,128)(2,1)S(1)} %bitcast.13, bf16[27,64,256]{2,1,0:T(8,128)(2,1)S(1)} %copy-done.2), custom_call_target="tpu_custom_call" | custom-call | tf_op jit(solution)/shard_map/gather_inputs/pallas_call | solution.py:325
  33.2 0.0 copy-start.4
  33.2 1.7 %copy-done.4 = bf16[27,256,256]{2,1,0:T(8,128)(2,1)} copy-done((bf16[27,256,256]{2,1,0:T(8,128)(2,1)}, bf16[27,256,256]{2,1,0:T(8,128)(2,1)S(1)}, u32[]{:S(2)}) %copy-start.4) | copy-done | bytes 3538968
  34.9 0.0 copy-start.5
  34.9 1.0 copy-done.5
  35.9 15.8 %pair_products.1 = (bf16[8,128,256]{2,1,0:T(8,128)(2,1)}, bf16[16,128,256]{2,1,0:T(8,128)(2,1)}, f32[8,128,256]{2,1,0:T(8,128)}, bf16[27,256,256]{2,1,0:T(8,128)(2,1)}) custom-call(s32[162]{0:T(256)} %reshape_squeeze.7.kmap_ref, s32[27]{0:T(128)} %bitcast.16, bf16[8,128,256]{2,1,0:T(8,128)(2,1)} %bitcast.12, bf16[16,128,256]{2,1,0:T(8,128)(2,1)} %copy-done.5, ...), custom_call_target="tpu_custom_call" | custom-call | flops 4076863488 | bytes 16777216 | tf_op jit(solution)/shard_map/pair_products/pallas_call | solution.py:68
  51.6 0.0 copy-start
  51.6 2.0 %copy-done = bf16[27,256,256]{2,1,0:T(8,128)(2,1)S(1)} copy-done((bf16[27,256,256]{2,1,0:T(8,128)(2,1)S(1)}, bf16[27,256,256]{2,1,0:T(8,128)(2,1)}, u32[]{:S(2)}) %copy-start) | copy-done | bytes 3538968
  53.6 0.0 copy-start.1
  53.6 1.2 copy-done.1
  54.9 70.1 %reduce_and_return.1 = (bf16[1792,256]{1,0:T(8,128)(2,1)S(1)}, bf16[16,128,256]{2,1,0:T(8,128)(2,1)S(1)}) custom-call(bf16[27,256,256]{2,1,0:T(8,128)(2,1)S(1)} %copy-done, bf16[16,128,256]{2,1,0:T(8,128)(2,1)S(1)} %copy-done.1), custom_call_target="tpu_custom_call" | custom-call | tf_op jit(solution)/shard_map/reduce_and_return/pallas_call | solution.py:213
  125.0 0.0 copy-start.6
  125.0 0.7 fusion.1
  125.7 0.5 copy-done.6
  126.2 1.1 fusion.3
  127.3 1.3 %convert_multiply_fusion = f32[1728,256]{1,0:T(8,128)} fusion(bf16[1792,256]{1,0:T(8,128)(2,1)S(1)} %get-tuple-element.18), kind=kLoop, calls=%fused_computation | loop fusion | flops 884736 | bytes 2654208 | tf_op jit(solution)/shard_map/div | solution.py:362
Async XLA Ops:
  3.0 1.2 copy-start.2
  4.1 1.0 copy-start.3
  33.2 1.7 %copy-start.4 = (bf16[27,256,256]{2,1,0:T(8,128)(2,1)}, bf16[27,256,256]{2,1,0:T(8,128)(2,1)S(1)}, u32[]{:S(2)}) copy-start(bf16[27,256,256]{2,1,0:T(8,128)(2,1)S(1)} %get-tuple-element.12.weights_ref) | copy-start | bytes 10616836
  34.9 1.0 copy-start.5
  51.6 2.0 %copy-start = (bf16[27,256,256]{2,1,0:T(8,128)(2,1)S(1)}, bf16[27,256,256]{2,1,0:T(8,128)(2,1)}, u32[]{:S(2)}) copy-start(bf16[27,256,256]{2,1,0:T(8,128)(2,1)} %get-tuple-element.15.wgrad_ref) | copy-start | bytes 10616836
  53.6 1.2 copy-start.1
  125.0 1.2 copy-start.6
